TPU v7x, 256 devices: a whole 4x4x8 slice. The times are simulated.
256 devices in a mesh: blk: 128 (over y_hi, z, x, core), rep: 2 (over y_lo).
Axes of the slice: x: 4, y: 4 (y_hi: 2, y_lo: 2; y = y_hi * 2 + y_lo), z: 8, core: 2. Of those that a mesh axis runs over, the one named last changes fastest.
Arguments:
- features: float32 [32768, 256], P('blk', 'rep'), may hold values from -6 to 6
- scaling: float32 [32768], P('blk'), may hold values from 0.5 to 2
- signal: float32 [64, 32768], P('rep', 'blk'), may hold values from -6 to 6
Outputs:
- diffused: float32 [64, 32768], P('rep', 'blk')
All inputs are finite; a program needn't handle non-finite values.
Results may differ from a plain program's by a relative error of at most 0.0003.
Values sent between devices are 32-bit elements; how exact they have to be, the bound alone decides.
No kernel may reach another device: no remote copies, remote signals or barrier semaphores. Data moves between devices by JAX's collectives and lax.ppermute only.
A program may use at most 64 MiB of HBM per device.

v0:
```python
import functools
import math

import jax
import jax.numpy as jnp
from jax import lax
from jax.experimental import pallas as pl
from jax.experimental.pallas import tpu as pltpu
from jax.sharding import Mesh
from jax.sharding import PartitionSpec as P

F32, BF16 = jnp.float32, jnp.bfloat16
LOG2E = 1.4426950408889634
SHARPNESS = 48.0
NT = (((1,), (1,)), ((), ()))
NN = (((1,), (0,)), ((), ()))
SM = pl.BlockSpec(memory_space=pltpu.SMEM)
AXES = ("yh", "z", "x", "co", "yl")
PLANE = ("yh", "x", "yl")
LINE = ("z", "co")
EXTRA = 40


def params(mib):
    return pltpu.CompilerParams(vmem_limit_bytes=mib * 2**20)


def split(value):
    high = value.astype(BF16)
    return high, (value - high.astype(F32)).astype(BF16)


def unit(full):
    mean_square = jnp.mean(full * full, axis=1, keepdims=True)
    return full * (lax.rsqrt(mean_square + 1e-06) * math.sqrt(SHARPNESS / full.shape[1]))


def whole(*shape):
    return pl.BlockSpec(shape, lambda i: (0,) * len(shape))


def pack_kernel(features_ref, scaling_ref, signal_ref, spread_ref, give_ref, kept_ref, message_ref, sems):
    message_ref[0:256, :] = features_ref[...]
    message_ref[256:258, :] = scaling_ref[...]
    message_ref[258:264, :] = jnp.zeros((6, 128), F32)
    copies = [pltpu.make_async_copy(message_ref, spread_ref.at[n], sems.at[n]) for n in range(16)]
    for copy in copies:
        copy.start()
    place = lax.axis_index("yl")
    for own in range(2):

        @pl.when(place == own)
        def _():
            for half, out in ((own, kept_ref), (1 - own, give_ref)):
                out[0:32, :] = signal_ref[:, half * 128 : (half + 1) * 128]
                out[32:160, :] = features_ref[half * 128 : (half + 1) * 128, :]

    for copy in copies:
        copy.wait()


def pack(features, scaling, signal):
    return pl.pallas_call(
        pack_kernel,
        grid=(1,),
        in_specs=[whole(256, 128), whole(2, 128), whole(32, 256)],
        out_specs=[pl.BlockSpec(memory_space=pltpu.HBM), whole(160, 128), whole(160, 128)],
        out_shape=[pltpu.HBM((16, 264, 128), F32)] + [jax.ShapeDtypeStruct((160, 128), F32)] * 2,
        scratch_shapes=[pltpu.VMEM((264, 128), F32), pltpu.SemaphoreType.DMA((16,))],
        compiler_params=params(62),
        cost_estimate=pl.CostEstimate(flops=100_000, bytes_accessed=2_500_000, transcendentals=0),
        name="pack",
    )(features, scaling, signal)


def gate_kernel(spread_ref, after_ref, out_ref):
    pass


def gate(spread, after):
    hbm = pl.BlockSpec(memory_space=pltpu.HBM)
    return pl.pallas_call(
        gate_kernel,
        in_specs=[hbm, pl.BlockSpec(memory_space=pl.ANY)],
        out_specs=hbm,
        out_shape=pltpu.HBM(spread.shape, F32),
        input_output_aliases={0: 0},
        compiler_params=params(62),
        cost_estimate=pl.CostEstimate(flops=100_000, bytes_accessed=2_500_000, transcendentals=0),
        name="gate",
    )(spread, after)


def block_rows(first, second):
    high, low = split(unit(jnp.concatenate([first[0:256, :], second[0:256, :]], axis=1)))
    return jnp.concatenate([high, low, high], axis=1)


def kernel_of(units, rows, own=None):
    kern = jnp.exp2(lax.dot_general(units, rows, NT, preferred_element_type=F32))
    if own is None:
        return kern
    col = lax.broadcasted_iota(jnp.int32, (128, 256), 0)
    row = lax.broadcasted_iota(jnp.int32, (128, 256), 1) - own
    return jnp.concatenate([jnp.where(row == col, 0.0, kern[:128]), kern[128:]], axis=0)


def tile_columns(place_ref, rows_ref, cols_ref, scale_ref, unit_ref, acc_ref, got_ref=None):
    has_self = got_ref is not None
    for b in range(8):
        high, low = split(unit(cols_ref[b, EXTRA:, :]) * LOG2E)
        at = slice(b * 128, (b + 1) * 128)
        unit_ref[at, 0:256] = high
        unit_ref[at, 256:512] = high
        unit_ref[at, 512:768] = low
    for c in range(8):
        at = slice(c * 256, (c + 1) * 256)
        if has_self:
            rows_ref[at, :] = block_rows(got_ref[2 * c], got_ref[2 * c + 1])
            scale_ref[2 * c : 2 * c + 2, :] = got_ref[2 * c, 256:258, :]
        kern = kernel_of(unit_ref[...], rows_ref[at, :], place_ref[0] - c * 256 if has_self else None)
        part = kern[:, :128] * scale_ref[2 * c : 2 * c + 1, :]
        part += kern[:, 128:] * scale_ref[2 * c + 1 : 2 * c + 2, :]
        acc_ref[...] = part if c == 0 else acc_ref[...] + part
    total = lax.dot_general(
        jnp.ones((8, 128), F32), acc_ref[...], NT, precision=lax.Precision.HIGHEST, preferred_element_type=F32
    )
    return [total[0:1, b * 128 : (b + 1) * 128] for b in range(8)]


def near_kernel(place_ref, got_ref, cols_ref, unit_ref, extra_ref, sum_ref, rows_ref, scale_ref, acc_ref):
    extra_ref[...] = cols_ref[:, 0:EXTRA, :]
    sums = tile_columns(place_ref, rows_ref, cols_ref, scale_ref, unit_ref, acc_ref, got_ref)
    for b in range(8):
        sum_ref[b : b + 1, :] = sums[b]


def far_kernel(place_ref, rows_ref, cols_ref, scale_ref, near_ref, unit_ref, extra_ref, spread_ref, acc_ref):
    extra_ref[...] = cols_ref[:, 0:EXTRA, :]
    sums = tile_columns(place_ref, rows_ref, cols_ref, scale_ref, unit_ref, acc_ref)
    first = place_ref[1] * 8
    for b in range(8):
        spread_ref[0, pl.ds(first + place_ref[2 + b], 1), :] = near_ref[b : b + 1, :]
        spread_ref[0, pl.ds(8 - first + place_ref[2 + b], 1), :] = sums[b]
    for n in range(1, 16):
        spread_ref[n] = spread_ref[0]


def tile(kernel, place, *arrays):
    vm = pl.BlockSpec(memory_space=pltpu.VMEM)
    shapes = [((1024, 768), BF16), ((8, EXTRA, 256), F32)]
    if kernel is near_kernel:
        shapes += [((8, 128), F32), ((2048, 768), BF16), ((16, 128), F32)]
    else:
        shapes += [((16, 16, 128), F32)]
    return pl.pallas_call(
        kernel,
        in_specs=[SM] + [vm] * len(arrays),
        out_specs=[vm] * len(shapes),
        out_shape=[jax.ShapeDtypeStruct(*shape) for shape in shapes],
        scratch_shapes=[pltpu.VMEM((1024, 128), F32)],
        compiler_params=params(16),
        cost_estimate=pl.CostEstimate(flops=3_200_000_000, bytes_accessed=14_000_000, transcendentals=2_000_000),
        name="tile_near" if kernel is near_kernel else "tile_far",
    )(place, *arrays)


def diffuse_kernel(
    place_ref, parts_ref, extra0, extra1, rows_ref, unit0, unit1,
    terms_ref, balanced_ref, weight_ref, sums_ref, held, out_ref, sems,
):
    copies = []
    for c in range(9):
        if c < 8:
            rows = rows_ref[c * 256 : (c + 1) * 256, :]
            for core, units in enumerate((unit0, unit1)):
                at = slice(core * 1024, (core + 1) * 1024)
                kern = kernel_of(units[...], rows, None if core else place_ref[0] - c * 256)
                held[c % 2, 0, at, :], held[c % 2, 1, at, :] = split(kern)
        if c == 0:
            sums_ref[...] = parts_ref[...].sum(0)
            first = place_ref[1] * 8
            for core, extra in enumerate((extra0, extra1)):
                base = first if core == 0 else 8 - first
                for b in range(8):
                    balanced = jnp.sqrt(extra[b, 32:33, 0:128] / sums_ref[pl.ds(base + place_ref[2 + b], 1), :])
                    if core == 0 and b == 0:
                        balanced_ref[...] = balanced
                    signal = jnp.concatenate([extra[b, 0:32, 0:128], extra[b, 0:32, 128:256]], axis=0)
                    start = core * 1024 + b * 128
                    for n, part in enumerate(split(signal * balanced)):
                        weight_ref[n * 64 : (n + 1) * 64, start : start + 128] = part
        if c > 0:
            slot = (c - 1) % 2
            lead = lax.dot_general(weight_ref[...], held[slot, 0], NN, preferred_element_type=F32)
            rest = lax.dot_general(weight_ref[0:64, :], held[slot, 1], NN, preferred_element_type=F32)
            total = lead[:64] + lead[64:] + rest
            out_ref[2 * c - 2] = total[:32]
            out_ref[2 * c - 1] = total[32:]
            pair = pl.ds(2 * c - 2, 2)
            copies.append(pltpu.make_async_copy(out_ref.at[pair], terms_ref.at[pair], sems.at[c - 1]))
            copies[-1].start()
    for copy in copies:
        copy.wait()


def diffuse(place, parts, extra0, extra1, rows, unit0, unit1):
    vm = pl.BlockSpec(memory_space=pltpu.VMEM)
    return pl.pallas_call(
        diffuse_kernel,
        in_specs=[SM] + [vm] * 6,
        out_specs=[pl.BlockSpec(memory_space=pltpu.HBM), vm],
        out_shape=[pltpu.HBM((16, 32, 256), F32), jax.ShapeDtypeStruct((1, 128), F32)],
        scratch_shapes=[
            pltpu.VMEM((128, 2048), BF16),
            pltpu.VMEM((16, 128), F32),
            pltpu.VMEM((2, 2, 2048, 256), BF16),
            pltpu.VMEM((16, 32, 256), F32),
            pltpu.SemaphoreType.DMA((8,)),
        ],
        compiler_params=params(28),
        cost_estimate=pl.CostEstimate(flops=3_200_000_000, bytes_accessed=18_000_000, transcendentals=0),
        name="diffuse",
    )(place, parts, extra0, extra1, rows, unit0, unit1)


def swapped(array, axis):
    return lax.ppermute(array, axis, [(0, 1), (1, 0)])


def to_all(array, axes, count):
    spread = jnp.broadcast_to(array[None], (count,) + array.shape)
    return lax.all_to_all(spread, axes, 0, 0, tiled=True)


def shifted(array, axis, by):
    length = lax.axis_size(axis)
    return lax.ppermute(array, axis, [(i, (i + by) % length) for i in range(length)])


def on_device(features, scaling, signal):
    yh, z, x, co, yl = (lax.axis_index(a) for a in AXES)
    lower = yl == 0
    offsets = (0, 4, -2, 2, -1, 3, 1, 5)
    place = [(yh * 4 + x) * 256 + yl * 128, co] + [(z + o) % 8 for o in offsets]
    place = jnp.stack(place).astype(jnp.int32)

    def ordered(a, b, axis):
        return jnp.concatenate([jnp.where(lower, a, b), jnp.where(lower, b, a)], axis=axis)

    spread, give, kept = pack(features, scaling.reshape(2, 128), signal)
    spread = gate(spread, give)
    rows_raw = lax.all_to_all(spread, PLANE, 0, 0, tiled=True)

    got = swapped(give, "yl")
    own_scaling = jnp.where(lower, scaling[:128], scaling[128:])
    both = ordered(kept, got, 1)
    filler = jnp.zeros((EXTRA - 32, 256), F32).at[0, :128].set(own_scaling)
    own = jnp.concatenate([both[:32], filler, both[32:]], axis=0)[None]

    opposite = shifted(own, "z", 4)
    ahead, behind = shifted(own, "z", 2), shifted(own, "z", -2)
    pair = jnp.concatenate([own, opposite], axis=0)
    up, down = shifted(pair, "z", 1), shifted(pair, "z", -1)
    cols_near = jnp.concatenate([pair, ahead, behind, up, down], axis=0)
    cols_far = swapped(cols_near, "co")

    unit0, extra0, near, rows, scale = tile(near_kernel, place, rows_raw, cols_near)
    unit1, extra1, parts = tile(far_kernel, place, rows, cols_far, scale, near)

    parts = lax.all_to_all(parts, LINE, 0, 0, tiled=True)
    terms, own_balanced = diffuse(place, parts, extra0, extra1, rows, unit0, unit1)
    other_balanced = swapped(own_balanced, "yl")
    arrived = lax.all_to_all(terms, PLANE, 0, 0, tiled=True)
    return arrived.sum(0) * ordered(own_balanced, other_balanced, 1)


def solution(mesh):
    fine = Mesh(mesh.devices.reshape(2, 8, 4, 2, 2), AXES)
    blk = ("yh", "z", "x", "co")
    return jax.shard_map(
        on_device,
        mesh=fine,
        in_specs=(P(blk, "yl"), P(blk), P("yl", blk)),
        out_specs=P("yl", blk),
        check_vma=False,
    )
```

profile of v0, /device:TPU:1, one launch (start us, length us, event | category | flops | bytes accessed | tf_op | source)
XLA Modules:
  0.0 99.6 jit_solution(2001323085074352751)
XLA Ops:
  0.0 3.1 %pack.1 = (f32[16,264,128]{2,1,0:T(8,128)}, f32[160,128]{1,0:T(8,128)}, f32[160,128]{1,0:T(8,128)}) custom-call(f32[256,128]{1,0:T(8,128)} %features_ref.1, f32[2,128]{1,0:T(2,128)} %bitcast.18, f32[32,256]{1,0:T(8,128)} %signal_ref.1), custom_call_target="tpu_custom_call" | custom-call | flops 100000 | bytes 2500000 | tf_op jit(solution)/shard_map/pack/pallas_call | solution.py:63
  3.1 2.2 %collective-permute-start = (f32[160,128]{1,0:T(8,128)}, f32[160,128]{1,0:T(8,128)S(1)}, u32[]{:S(2)}, u32[]{:S(2)}) collective-permute-start(f32[160,128]{1,0:T(8,128)} %get-tuple-element.31.after_ref), channel_id=1, source_target_pairs={{0,1},{1,0},{2,3},{3,2},{4,5},{5,4},{6,7},{7,6},{8,9},{9,8},{10,11... | collective-permute-start | bytes 245768 | tf_op jit(solution)/shard_map/ppermute | solution.py:228
  5.3 0.0 copy-start.1
  5.3 0.0 copy-start
  5.3 6.6 %all-to-all-start = ((f32[16,264,128]{2,1,0:T(8,128)}), f32[16,264,128]{2,1,0:T(8,128)S(1)}, u32[]{:S(2)}, u32[]{:S(2)}) async-start(f32[16,264,128]{2,1,0:T(8,128)} %gate.1), calls=%async_computation | async-start | bytes 4325376 | tf_op jit(solution)/shard_map/all_to_all | solution.py:253
  11.9 0.0 copy-done.1
  11.9 0.0 collective-permute-done
  12.0 0.0 copy-done
  12.0 7.0 %collective-permute-start.1 = (f32[1,168,256]{2,1,0:T(8,128)S(1)}, f32[1,168,256]{2,1,0:T(8,128)S(1)}, u32[]{:S(2)}, u32[]{:S(2)}) collective-permute-start(f32[1,168,256]{2,1,0:T(8,128)S(1)} %fusion.1), channel_id=1, source_target_pairs={{0,64},{16,80},{32,96},{48,112},{64,0},{80,16},{96,32},{112,48},{1... | collective-permute-start | bytes 516104 | tf_op jit(solution)/shard_map/ppermute | solution.py:238
  19.0 1.2 %collective-permute-start.2 = (f32[1,168,256]{2,1,0:T(8,128)S(1)}, f32[1,168,256]{2,1,0:T(8,128)S(1)}, u32[]{:S(2)}, u32[]{:S(2)}) collective-permute-start(f32[1,168,256]{2,1,0:T(8,128)S(1)} %fusion.1), channel_id=1, source_target_pairs={{0,32},{16,48},{32,64},{48,80},{64,96},{80,112},{96,0},{112,16},{1... | collective-permute-start | bytes 516104 | tf_op jit(solution)/shard_map/ppermute | solution.py:238
  20.2 2.4 %collective-permute-start.3 = (f32[1,168,256]{2,1,0:T(8,128)S(1)}, f32[1,168,256]{2,1,0:T(8,128)S(1)}, u32[]{:S(2)}, u32[]{:S(2)}) collective-permute-start(f32[1,168,256]{2,1,0:T(8,128)S(1)} %fusion.1), channel_id=1, source_target_pairs={{0,96},{16,112},{32,0},{48,16},{64,32},{80,48},{96,64},{112,80},{1... | collective-permute-start | bytes 516104 | tf_op jit(solution)/shard_map/ppermute | solution.py:238
  22.6 0.0 collective-permute-done.1
  22.6 3.8 %collective-permute-start.4 = (f32[2,168,256]{2,1,0:T(8,128)S(1)}, f32[2,168,256]{2,1,0:T(8,128)S(1)}, u32[]{:S(2)}, u32[]{:S(2)}) collective-permute-start(f32[2,168,256]{2,1,0:T(8,128)S(1)} %pad_maximum_fusion), channel_id=1, source_target_pairs={{0,16},{16,32},{32,48},{48,64},{64,80},{80,96},{96,112},{112,0},{1... | collective-permute-start | bytes 1032200 | tf_op jit(solution)/shard_map/ppermute | solution.py:238
  26.5 2.0 %collective-permute-start.5 = (f32[2,168,256]{2,1,0:T(8,128)S(1)}, f32[2,168,256]{2,1,0:T(8,128)S(1)}, u32[]{:S(2)}, u32[]{:S(2)}) collective-permute-start(f32[2,168,256]{2,1,0:T(8,128)S(1)} %pad_maximum_fusion), channel_id=1, source_target_pairs={{0,112},{16,0},{32,16},{48,32},{64,48},{80,64},{96,80},{112,96},{1... | collective-permute-start | bytes 1032200 | tf_op jit(solution)/shard_map/ppermute | solution.py:238
  28.5 2.5 %collective-permute-done.2 = f32[1,168,256]{2,1,0:T(8,128)S(1)} collective-permute-done((f32[1,168,256]{2,1,0:T(8,128)S(1)}, f32[1,168,256]{2,1,0:T(8,128)S(1)}, u32[]{:S(2)}, u32[]{:S(2)}) %collective-permute-start.2) | collective-permute-done | bytes 172064 | tf_op jit(solution)/shard_map/ppermute | solution.py:238
  31.0 4.2 %collective-permute-done.3 = f32[1,168,256]{2,1,0:T(8,128)S(1)} collective-permute-done((f32[1,168,256]{2,1,0:T(8,128)S(1)}, f32[1,168,256]{2,1,0:T(8,128)S(1)}, u32[]{:S(2)}, u32[]{:S(2)}) %collective-permute-start.3) | collective-permute-done | bytes 172064 | tf_op jit(solution)/shard_map/ppermute | solution.py:238
  35.2 6.2 %collective-permute-done.4 = f32[2,168,256]{2,1,0:T(8,128)S(1)} collective-permute-done((f32[2,168,256]{2,1,0:T(8,128)S(1)}, f32[2,168,256]{2,1,0:T(8,128)S(1)}, u32[]{:S(2)}, u32[]{:S(2)}) %collective-permute-start.4) | collective-permute-done | bytes 344096 | tf_op jit(solution)/shard_map/ppermute | solution.py:238
  41.3 0.7 collective-permute-done.5
  42.0 1.6 %collective-permute-start.6 = (f32[8,168,256]{2,1,0:T(8,128)S(1)}, f32[8,168,256]{2,1,0:T(8,128)}, u32[]{:S(2)}, u32[]{:S(2)}) collective-permute-start(f32[8,168,256]{2,1,0:T(8,128)S(1)} %constant_dynamic-update-slice_fusion.cols_ref), channel_id=1, source_target_pairs={{0,2},{2,0},{1,3},{3,1},{4,6},{6,4},{5,7},{7,5},{8,10},{10,8},{9,1... | collective-permute-start | bytes 4128776 | tf_op jit(solution)/shard_map/ppermute | solution.py:228
  43.6 0.1 stack.43.place_ref
  43.7 0.0 all-to-all-done.got_ref
  43.7 4.7 %tile_near.1 = (bf16[1024,768]{1,0:T(8,128)(2,1)S(1)}, f32[8,40,256]{2,1,0:T(8,128)S(1)}, f32[8,128]{1,0:T(8,128)S(1)}, bf16[2048,768]{1,0:T(8,128)(2,1)S(1)}, f32[16,128]{1,0:T(8,128)S(1)}) custom-call(s32[10]{0:T(128)S(1)} %stack.43.place_ref, f32[16,264,128]{2,1,0:T(8,128)S(1)} %all-to-all-done.got_ref, ...), custom_call_target="tpu_custom_call" | custom-call | flops 3200000000 | bytes 14000000 | tf_op jit(solution)/shard_map/tile_near/pallas_call | solution.py:156
  48.4 0.0 collective-permute-done.6.cols_ref
  48.4 5.4 %tile_far.1 = (bf16[1024,768]{1,0:T(8,128)(2,1)S(1)}, f32[8,40,256]{2,1,0:T(8,128)S(1)}, f32[16,16,128]{2,1,0:T(8,128)S(1)}) custom-call(s32[10]{0:T(128)S(1)} %stack.43.place_ref, bf16[2048,768]{1,0:T(8,128)(2,1)S(1)} %get-tuple-element.33.rows_ref, f32[8,168,256]{2,1,0:T(8,128)} %collective-permute-done.6.cols_ref, ...), custom_call_target="tpu_custom_call" | custom-call | flops 3200000000 | bytes 14000000 | tf_op jit(solution)/shard_map/tile_far/pallas_call | solution.py:156
  53.7 18.5 %all_to_all.15.parts_ref = f32[16,16,128]{2,1,0:T(8,128)S(1)} all-to-all(f32[16,16,128]{2,1,0:T(8,128)S(1)} %get-tuple-element.36), channel_id=1, replica_groups=mesh['yh'=2,'z'=8,'x'=4,'co'=2,'yl'=2] {'z','co'}, dimensions={0} | all-to-all | bytes 262144 | tf_op jit(solution)/shard_map/all_to_all | solution.py:271
  72.3 11.0 %diffuse.1 = (f32[16,32,256]{2,1,0:T(8,128)}, f32[1,128]{1,0:T(1,128)S(1)}) custom-call(s32[10]{0:T(128)S(1)} %stack.43.place_ref, f32[16,16,128]{2,1,0:T(8,128)S(1)} %all_to_all.15.parts_ref, f32[8,40,256]{2,1,0:T(8,128)S(1)} %get-tuple-element.37.extra0, f32[8,40,256]{2,1,0:T(8,128)S(1)} %get-tuple-element.38.extra1, ...), custom_call_target="tpu_custom_call" | custom-call | flops 3200000000 | bytes 18000000 | tf_op jit(solution)/shard_map/diffuse/pallas_call | solution.py:209
  83.3 3.6 %all-to-all-start.2 = ((f32[16,32,256]{2,1,0:T(8,128)}), f32[16,32,256]{2,1,0:T(8,128)S(1)}, u32[]{:S(2)}, u32[]{:S(2)}) async-start(f32[16,32,256]{2,1,0:T(8,128)} %get-tuple-element.41), calls=%async_computation.2 | async-start | bytes 1048576 | tf_op jit(solution)/shard_map/all_to_all | solution.py:274
  86.9 1.2 %collective-permute-start.7 = (f32[1,128]{1,0:T(1,128)S(1)}, f32[1,128]{1,0:T(1,128)S(1)}, u32[]{:S(2)}, u32[]{:S(2)}) collective-permute-start(f32[1,128]{1,0:T(1,128)S(1)} %get-tuple-element.42), channel_id=1, source_target_pairs={{0,1},{1,0},{2,3},{3,2},{4,5},{5,4},{6,7},{7,6},{8,9},{9,8},{10,11... | collective-permute-start | bytes 1544 | tf_op jit(solution)/shard_map/ppermute | solution.py:228
  88.1 2.7 %collective-permute-done.7 = f32[1,128]{1,0:T(1,128)S(1)} collective-permute-done((f32[1,128]{1,0:T(1,128)S(1)}, f32[1,128]{1,0:T(1,128)S(1)}, u32[]{:S(2)}, u32[]{:S(2)}) %collective-permute-start.7) | collective-permute-done | bytes 544 | tf_op jit(solution)/shard_map/ppermute | solution.py:228
  90.8 8.1 %all-to-all-done.2 = f32[16,32,256]{2,1,0:T(8,128)S(1)} async-done(((f32[16,32,256]{2,1,0:T(8,128)}), f32[16,32,256]{2,1,0:T(8,128)S(1)}, u32[]{:S(2)}, u32[]{:S(2)}) %all-to-all-start.2) | async-done | bytes 524320 | tf_op jit(solution)/shard_map/all_to_all | solution.py:274
  99.0 0.6 broadcast_multiply_fusion
  (14 shorter events, 0.2 us)
Async XLA Ops:
  3.1 8.9 %collective-permute-start = (f32[160,128]{1,0:T(8,128)}, f32[160,128]{1,0:T(8,128)S(1)}, u32[]{:S(2)}, u32[]{:S(2)}) collective-permute-start(f32[160,128]{1,0:T(8,128)} %get-tuple-element.31.after_ref), channel_id=1, source_target_pairs={{0,1},{1,0},{2,3},{3,2},{4,5},{5,4},{6,7},{7,6},{8,9},{9,8},{10,11... | collective-permute-start | bytes 245768 | tf_op jit(solution)/shard_map/ppermute | solution.py:228
  5.3 6.6 %copy-start.1 = (f32[256]{0:T(256)S(1)}, f32[256]{0:T(256)}, u32[]{:S(2)}) copy-start(f32[256]{0:T(256)} %param.6) | copy-start | bytes 3076
  5.3 6.6 %copy-start = (f32[160,128]{1,0:T(8,128)S(1)}, f32[160,128]{1,0:T(8,128)}, u32[]{:S(2)}) copy-start(f32[160,128]{1,0:T(8,128)} %get-tuple-element.32) | copy-start | bytes 245764
  5.3 38.4 %all-to-all-start = ((f32[16,264,128]{2,1,0:T(8,128)}), f32[16,264,128]{2,1,0:T(8,128)S(1)}, u32[]{:S(2)}, u32[]{:S(2)}) async-start(f32[16,264,128]{2,1,0:T(8,128)} %gate.1), calls=%async_computation | async-start | bytes 4325376 | tf_op jit(solution)/shard_map/all_to_all | solution.py:253
  12.0 10.6 %collective-permute-start.1 = (f32[1,168,256]{2,1,0:T(8,128)S(1)}, f32[1,168,256]{2,1,0:T(8,128)S(1)}, u32[]{:S(2)}, u32[]{:S(2)}) collective-permute-start(f32[1,168,256]{2,1,0:T(8,128)S(1)} %fusion.1), channel_id=1, source_target_pairs={{0,64},{16,80},{32,96},{48,112},{64,0},{80,16},{96,32},{112,48},{1... | collective-permute-start | bytes 516104 | tf_op jit(solution)/shard_map/ppermute | solution.py:238
  19.0 11.9 %collective-permute-start.2 = (f32[1,168,256]{2,1,0:T(8,128)S(1)}, f32[1,168,256]{2,1,0:T(8,128)S(1)}, u32[]{:S(2)}, u32[]{:S(2)}) collective-permute-start(f32[1,168,256]{2,1,0:T(8,128)S(1)} %fusion.1), channel_id=1, source_target_pairs={{0,32},{16,48},{32,64},{48,80},{64,96},{80,112},{96,0},{112,16},{1... | collective-permute-start | bytes 516104 | tf_op jit(solution)/shard_map/ppermute | solution.py:238
  20.2 14.9 %collective-permute-start.3 = (f32[1,168,256]{2,1,0:T(8,128)S(1)}, f32[1,168,256]{2,1,0:T(8,128)S(1)}, u32[]{:S(2)}, u32[]{:S(2)}) collective-permute-start(f32[1,168,256]{2,1,0:T(8,128)S(1)} %fusion.1), channel_id=1, source_target_pairs={{0,96},{16,112},{32,0},{48,16},{64,32},{80,48},{96,64},{112,80},{1... | collective-permute-start | bytes 516104 | tf_op jit(solution)/shard_map/ppermute | solution.py:238
  22.6 18.7 %collective-permute-start.4 = (f32[2,168,256]{2,1,0:T(8,128)S(1)}, f32[2,168,256]{2,1,0:T(8,128)S(1)}, u32[]{:S(2)}, u32[]{:S(2)}) collective-permute-start(f32[2,168,256]{2,1,0:T(8,128)S(1)} %pad_maximum_fusion), channel_id=1, source_target_pairs={{0,16},{16,32},{32,48},{48,64},{64,80},{80,96},{96,112},{112,0},{1... | collective-permute-start | bytes 1032200 | tf_op jit(solution)/shard_map/ppermute | solution.py:238
  26.5 15.5 %collective-permute-start.5 = (f32[2,168,256]{2,1,0:T(8,128)S(1)}, f32[2,168,256]{2,1,0:T(8,128)S(1)}, u32[]{:S(2)}, u32[]{:S(2)}) collective-permute-start(f32[2,168,256]{2,1,0:T(8,128)S(1)} %pad_maximum_fusion), channel_id=1, source_target_pairs={{0,112},{16,0},{32,16},{48,32},{64,48},{80,64},{96,80},{112,96},{1... | collective-permute-start | bytes 1032200 | tf_op jit(solution)/shard_map/ppermute | solution.py:238
  42.0 6.3 %collective-permute-start.6 = (f32[8,168,256]{2,1,0:T(8,128)S(1)}, f32[8,168,256]{2,1,0:T(8,128)}, u32[]{:S(2)}, u32[]{:S(2)}) collective-permute-start(f32[8,168,256]{2,1,0:T(8,128)S(1)} %constant_dynamic-update-slice_fusion.cols_ref), channel_id=1, source_target_pairs={{0,2},{2,0},{1,3},{3,1},{4,6},{6,4},{5,7},{7,5},{8,10},{10,8},{9,1... | collective-permute-start | bytes 4128776 | tf_op jit(solution)/shard_map/ppermute | solution.py:228
  83.3 15.7 %all-to-all-start.2 = ((f32[16,32,256]{2,1,0:T(8,128)}), f32[16,32,256]{2,1,0:T(8,128)S(1)}, u32[]{:S(2)}, u32[]{:S(2)}) async-start(f32[16,32,256]{2,1,0:T(8,128)} %get-tuple-element.41), calls=%async_computation.2 | async-start | bytes 1048576 | tf_op jit(solution)/shard_map/all_to_all | solution.py:274
  86.9 3.9 %collective-permute-start.7 = (f32[1,128]{1,0:T(1,128)S(1)}, f32[1,128]{1,0:T(1,128)S(1)}, u32[]{:S(2)}, u32[]{:S(2)}) collective-permute-start(f32[1,128]{1,0:T(1,128)S(1)} %get-tuple-element.42), channel_id=1, source_target_pairs={{0,1},{1,0},{2,3},{3,2},{4,5},{5,4},{6,7},{7,6},{8,9},{9,8},{10,11... | collective-permute-start | bytes 1544 | tf_op jit(solution)/shard_map/ppermute | solution.py:228
where the time goes:
time: 100 us; the launch traced here: 99.6 us
  starting transfers between devices  31.6 us (32%)
  waiting for transfers between devices  24.3 us (24%)
  Pallas kernels  24.1 us (24%)
  blocking collectives  18.5 us (18%)
    all_to_all x1, blocking collectives, on_device(): parts = lax.all_to_all(parts, LINE, 0, 0, tiled=True)  18.5 us
    ppermute x5, starting transfers between devices, shifted(): lax.ppermute(array, axis, [(i, (i + by) % length) for i in range(length)])  16.4 us
    ppermute x5, waiting for transfers between devices, shifted(): lax.ppermute(array, axis, [(i, (i + by) % length) for i in range(length)])  13.5 us
    pallas_call x1, Pallas kernels, diffuse(): pl.pallas_call(diffuse_kernel, in_specs=[SM] + [vm] * 6, out_specs=[pl.Bl...  11 us
    pallas_call x2, Pallas kernels, tile(): pl.pallas_call(kernel, in_specs=[SM] + [vm] * len(arrays), out_specs=[vm]...  10 us
    all_to_all x1, waiting for transfers between devices, on_device(): arrived = lax.all_to_all(terms, PLANE, 0, 0, tiled=True)  8.1 us
    all_to_all x1, starting transfers between devices, on_device(): rows_raw = lax.all_to_all(spread, PLANE, 0, 0, tiled=True)  6.59 us
    ppermute x3, starting transfers between devices, swapped(): return lax.ppermute(array, axis, [(0, 1), (1, 0)])  5.04 us
  transfers between devices with their start and end apart: 10, of which 6 were waited for; matrix products, arithmetic and copies ran while one was open for 0% of the time, Pallas kernels for 5%

commit v1 on v0

--- a/solution.py
+++ b/solution.py
@@ -241,7 +241,7 @@
 def on_device(features, scaling, signal):
     yh, z, x, co, yl = (lax.axis_index(a) for a in AXES)
     lower = yl == 0
-    offsets = (0, 4, -2, 2, -1, 3, 1, 5)
+    offsets = (0, 4, -1, 1, -2, -3, 2, 3)
     place = [(yh * 4 + x) * 256 + yl * 128, co] + [(z + o) % 8 for o in offsets]
     place = jnp.stack(place).astype(jnp.int32)
 
@@ -258,11 +258,11 @@
     filler = jnp.zeros((EXTRA - 32, 256), F32).at[0, :128].set(own_scaling)
     own = jnp.concatenate([both[:32], filler, both[32:]], axis=0)[None]
 
+    up, down = shifted(own, "z", 1), shifted(own, "z", -1)
     opposite = shifted(own, "z", 4)
-    ahead, behind = shifted(own, "z", 2), shifted(own, "z", -2)
-    pair = jnp.concatenate([own, opposite], axis=0)
-    up, down = shifted(pair, "z", 1), shifted(pair, "z", -1)
-    cols_near = jnp.concatenate([pair, ahead, behind, up, down], axis=0)
+    ahead = shifted(jnp.concatenate([own, up], axis=0), "z", 2)
+    behind = shifted(jnp.concatenate([own, down], axis=0), "z", -2)
+    cols_near = jnp.concatenate([own, opposite, up, down, ahead, behind], axis=0)
     cols_far = swapped(cols_near, "co")
 
     unit0, extra0, near, rows, scale = tile(near_kernel, place, rows_raw, cols_near)

time: 100 us -> 103 us (1.030)
  starting transfers between devices: 31.6 us -> 35.6 us
    ppermute x3, starting transfers between devices: 5.04 us -> 8.85 us  [swapped(): return lax.ppermute(array, axis, [(0, 1), (1, 0)])]
    all_to_all x1, starting transfers between devices: 3.58 us -> 6.81 us  [on_device(): arrived = lax.all_to_all(terms, PLANE, 0, 0, tiled=True)]
    ppermute x5, starting transfers between devices: 16.4 us -> 13.3 us  [shifted(): lax.ppermute(array, axis, [(i, (i + by) % length) for i in range(length)])]
  transfers between devices with their start and end apart: 10 -> 10, of which waited for: 6 -> 5; matrix products, arithmetic and copies ran while one was open for 0% -> 0% of each run, Pallas kernels for 5% -> 5%
where the time goes in v1:
time: 103 us; the launch traced here: 102 us
  starting transfers between devices  35.6 us (35%)
  Pallas kernels  24.1 us (23%)
  waiting for transfers between devices  23.6 us (23%)
  blocking collectives  18 us (17%)
    all_to_all x1, blocking collectives, on_device(): parts = lax.all_to_all(parts, LINE, 0, 0, tiled=True)  18 us
    ppermute x5, waiting for transfers between devices, shifted(): lax.ppermute(array, axis, [(i, (i + by) % length) for i in range(length)])  13.4 us
    ppermute x5, starting transfers between devices, shifted(): lax.ppermute(array, axis, [(i, (i + by) % length) for i in range(length)])  13.3 us
    pallas_call x1, Pallas kernels, diffuse(): pl.pallas_call(diffuse_kernel, in_specs=[SM] + [vm] * 6, out_specs=[pl.Bl...  11 us
    pallas_call x2, Pallas kernels, tile(): pl.pallas_call(kernel, in_specs=[SM] + [vm] * len(arrays), out_specs=[vm]...  10 us
    ppermute x3, starting transfers between devices, swapped(): return lax.ppermute(array, axis, [(0, 1), (1, 0)])  8.85 us
    all_to_all x1, waiting for transfers between devices, on_device(): arrived = lax.all_to_all(terms, PLANE, 0, 0, tiled=True)  7.62 us
    all_to_all x1, starting transfers between devices, on_device(): arrived = lax.all_to_all(terms, PLANE, 0, 0, tiled=True)  6.81 us
  transfers between devices with their start and end apart: 10, of which 5 were waited for; matrix products, arithmetic and copies ran while one was open for 0% of the time, Pallas kernels for 5%

profile of v1, /device:TPU:1, one launch (start us, length us, event | category | flops | bytes accessed | tf_op | source)
XLA Modules:
  0.0 102.4 jit_solution(14833221845210531351)
XLA Ops:
  0.0 3.1 %pack.1 = (f32[16,264,128]{2,1,0:T(8,128)}, f32[160,128]{1,0:T(8,128)}, f32[160,128]{1,0:T(8,128)}) custom-call(f32[256,128]{1,0:T(8,128)} %features_ref.1, f32[2,128]{1,0:T(2,128)} %bitcast.18, f32[32,256]{1,0:T(8,128)} %signal_ref.1), custom_call_target="tpu_custom_call" | custom-call | flops 100000 | bytes 2500000 | tf_op jit(solution)/shard_map/pack/pallas_call | solution.py:63
  3.1 2.2 %collective-permute-start = (f32[160,128]{1,0:T(8,128)}, f32[160,128]{1,0:T(8,128)S(1)}, u32[]{:S(2)}, u32[]{:S(2)}) collective-permute-start(f32[160,128]{1,0:T(8,128)} %get-tuple-element.31.after_ref), channel_id=1, source_target_pairs={{0,1},{1,0},{2,3},{3,2},{4,5},{5,4},{6,7},{7,6},{8,9},{9,8},{10,11... | collective-permute-start | bytes 245768 | tf_op jit(solution)/shard_map/ppermute | solution.py:228
  5.3 0.0 copy-start.1
  5.3 0.0 copy-start
  5.3 6.6 %all-to-all-start = ((f32[16,264,128]{2,1,0:T(8,128)}), f32[16,264,128]{2,1,0:T(8,128)S(1)}, u32[]{:S(2)}, u32[]{:S(2)}) async-start(f32[16,264,128]{2,1,0:T(8,128)} %gate.1), calls=%async_computation | async-start | bytes 4325376 | tf_op jit(solution)/shard_map/all_to_all | solution.py:253
  11.9 0.0 copy-done.1
  12.0 0.0 collective-permute-done
  12.0 0.0 copy-done
  12.0 1.7 %collective-permute-start.2 = (f32[1,168,256]{2,1,0:T(8,128)S(1)}, f32[1,168,256]{2,1,0:T(8,128)S(1)}, u32[]{:S(2)}, u32[]{:S(2)}) collective-permute-start(f32[1,168,256]{2,1,0:T(8,128)S(1)} %fusion.1), channel_id=1, source_target_pairs={{0,16},{16,32},{32,48},{48,64},{64,80},{80,96},{96,112},{112,0},{1... | collective-permute-start | bytes 516104 | tf_op jit(solution)/shard_map/ppermute | solution.py:238
  13.7 4.0 %collective-permute-start.3 = (f32[1,168,256]{2,1,0:T(8,128)S(1)}, f32[1,168,256]{2,1,0:T(8,128)S(1)}, u32[]{:S(2)}, u32[]{:S(2)}) collective-permute-start(f32[1,168,256]{2,1,0:T(8,128)S(1)} %fusion.1), channel_id=1, source_target_pairs={{0,112},{16,0},{32,16},{48,32},{64,48},{80,64},{96,80},{112,96},{1... | collective-permute-start | bytes 516104 | tf_op jit(solution)/shard_map/ppermute | solution.py:238
  17.8 3.9 %collective-permute-start.1 = (f32[1,168,256]{2,1,0:T(8,128)S(1)}, f32[1,168,256]{2,1,0:T(8,128)S(1)}, u32[]{:S(2)}, u32[]{:S(2)}) collective-permute-start(f32[1,168,256]{2,1,0:T(8,128)S(1)} %fusion.1), channel_id=1, source_target_pairs={{0,64},{16,80},{32,96},{48,112},{64,0},{80,16},{96,32},{112,48},{1... | collective-permute-start | bytes 516104 | tf_op jit(solution)/shard_map/ppermute | solution.py:238
  21.7 0.0 collective-permute-done.2
  21.7 0.0 collective-permute-done.3
  21.7 0.1 pad_maximum_fusion
  21.8 1.1 %collective-permute-start.4 = (f32[2,168,256]{2,1,0:T(8,128)S(1)}, f32[2,168,256]{2,1,0:T(8,128)S(1)}, u32[]{:S(2)}, u32[]{:S(2)}) collective-permute-start(f32[2,168,256]{2,1,0:T(8,128)S(1)} %get-tuple-element.44), channel_id=1, source_target_pairs={{0,32},{16,48},{32,64},{48,80},{64,96},{80,112},{96,0},{112,16},{1... | collective-permute-start | bytes 1032200 | tf_op jit(solution)/shard_map/ppermute | solution.py:238
  22.9 2.6 %collective-permute-start.5 = (f32[2,168,256]{2,1,0:T(8,128)S(1)}, f32[2,168,256]{2,1,0:T(8,128)S(1)}, u32[]{:S(2)}, u32[]{:S(2)}) collective-permute-start(f32[2,168,256]{2,1,0:T(8,128)S(1)} %get-tuple-element.43), channel_id=1, source_target_pairs={{0,96},{16,112},{32,0},{48,16},{64,32},{80,48},{96,64},{112,80},{1... | collective-permute-start | bytes 1032200 | tf_op jit(solution)/shard_map/ppermute | solution.py:238
  25.4 4.0 %collective-permute-done.1 = f32[1,168,256]{2,1,0:T(8,128)S(1)} collective-permute-done((f32[1,168,256]{2,1,0:T(8,128)S(1)}, f32[1,168,256]{2,1,0:T(8,128)S(1)}, u32[]{:S(2)}, u32[]{:S(2)}) %collective-permute-start.1) | collective-permute-done | bytes 172064 | tf_op jit(solution)/shard_map/ppermute | solution.py:238
  29.5 5.4 %collective-permute-done.4 = f32[2,168,256]{2,1,0:T(8,128)S(1)} collective-permute-done((f32[2,168,256]{2,1,0:T(8,128)S(1)}, f32[2,168,256]{2,1,0:T(8,128)S(1)}, u32[]{:S(2)}, u32[]{:S(2)}) %collective-permute-start.4) | collective-permute-done | bytes 344096 | tf_op jit(solution)/shard_map/ppermute | solution.py:238
  35.0 4.0 %collective-permute-done.5 = f32[2,168,256]{2,1,0:T(8,128)S(1)} collective-permute-done((f32[2,168,256]{2,1,0:T(8,128)S(1)}, f32[2,168,256]{2,1,0:T(8,128)S(1)}, u32[]{:S(2)}, u32[]{:S(2)}) %collective-permute-start.5) | collective-permute-done | bytes 344096 | tf_op jit(solution)/shard_map/ppermute | solution.py:238
  39.0 5.3 %collective-permute-start.6 = (f32[8,168,256]{2,1,0:T(8,128)S(1)}, f32[8,168,256]{2,1,0:T(8,128)}, u32[]{:S(2)}, u32[]{:S(2)}) collective-permute-start(f32[8,168,256]{2,1,0:T(8,128)S(1)} %constant_dynamic-update-slice_fusion.cols_ref), channel_id=1, source_target_pairs={{0,2},{2,0},{1,3},{3,1},{4,6},{6,4},{5,7},{7,5},{8,10},{10,8},{9,1... | collective-permute-start | bytes 4128776 | tf_op jit(solution)/shard_map/ppermute | solution.py:228
  44.3 0.1 stack.43.place_ref
  44.4 0.0 all-to-all-done.got_ref
  44.4 4.7 %tile_near.1 = (bf16[1024,768]{1,0:T(8,128)(2,1)S(1)}, f32[8,40,256]{2,1,0:T(8,128)S(1)}, f32[8,128]{1,0:T(8,128)S(1)}, bf16[2048,768]{1,0:T(8,128)(2,1)S(1)}, f32[16,128]{1,0:T(8,128)S(1)}) custom-call(s32[10]{0:T(128)S(1)} %stack.43.place_ref, f32[16,264,128]{2,1,0:T(8,128)S(1)} %all-to-all-done.got_ref, ...), custom_call_target="tpu_custom_call" | custom-call | flops 3200000000 | bytes 14000000 | tf_op jit(solution)/shard_map/tile_near/pallas_call | solution.py:156
  49.0 0.0 collective-permute-done.6.cols_ref
  49.0 5.3 %tile_far.1 = (bf16[1024,768]{1,0:T(8,128)(2,1)S(1)}, f32[8,40,256]{2,1,0:T(8,128)S(1)}, f32[16,16,128]{2,1,0:T(8,128)S(1)}) custom-call(s32[10]{0:T(128)S(1)} %stack.43.place_ref, bf16[2048,768]{1,0:T(8,128)(2,1)S(1)} %get-tuple-element.33.rows_ref, f32[8,168,256]{2,1,0:T(8,128)} %collective-permute-done.6.cols_ref, ...), custom_call_target="tpu_custom_call" | custom-call | flops 3200000000 | bytes 14000000 | tf_op jit(solution)/shard_map/tile_far/pallas_call | solution.py:156
  54.4 18.0 %all_to_all.15.parts_ref = f32[16,16,128]{2,1,0:T(8,128)S(1)} all-to-all(f32[16,16,128]{2,1,0:T(8,128)S(1)} %get-tuple-element.36), channel_id=1, replica_groups=mesh['yh'=2,'z'=8,'x'=4,'co'=2,'yl'=2] {'z','co'}, dimensions={0} | all-to-all | bytes 262144 | tf_op jit(solution)/shard_map/all_to_all | solution.py:271
  72.4 11.0 %diffuse.1 = (f32[16,32,256]{2,1,0:T(8,128)}, f32[1,128]{1,0:T(1,128)S(1)}) custom-call(s32[10]{0:T(128)S(1)} %stack.43.place_ref, f32[16,16,128]{2,1,0:T(8,128)S(1)} %all_to_all.15.parts_ref, f32[8,40,256]{2,1,0:T(8,128)S(1)} %get-tuple-element.37.extra0, f32[8,40,256]{2,1,0:T(8,128)S(1)} %get-tuple-element.38.extra1, ...), custom_call_target="tpu_custom_call" | custom-call | flops 3200000000 | bytes 18000000 | tf_op jit(solution)/shard_map/diffuse/pallas_call | solution.py:209
  83.4 6.8 %all-to-all-start.2 = ((f32[16,32,256]{2,1,0:T(8,128)}), f32[16,32,256]{2,1,0:T(8,128)S(1)}, u32[]{:S(2)}, u32[]{:S(2)}) async-start(f32[16,32,256]{2,1,0:T(8,128)} %get-tuple-element.41), calls=%async_computation.2 | async-start | bytes 1048576 | tf_op jit(solution)/shard_map/all_to_all | solution.py:274
  90.3 1.4 %collective-permute-start.7 = (f32[1,128]{1,0:T(1,128)S(1)}, f32[1,128]{1,0:T(1,128)S(1)}, u32[]{:S(2)}, u32[]{:S(2)}) collective-permute-start(f32[1,128]{1,0:T(1,128)S(1)} %get-tuple-element.42), channel_id=1, source_target_pairs={{0,1},{1,0},{2,3},{3,2},{4,5},{5,4},{6,7},{7,6},{8,9},{9,8},{10,11... | collective-permute-start | bytes 1544 | tf_op jit(solution)/shard_map/ppermute | solution.py:228
  91.6 2.5 %collective-permute-done.7 = f32[1,128]{1,0:T(1,128)S(1)} collective-permute-done((f32[1,128]{1,0:T(1,128)S(1)}, f32[1,128]{1,0:T(1,128)S(1)}, u32[]{:S(2)}, u32[]{:S(2)}) %collective-permute-start.7) | collective-permute-done | bytes 544 | tf_op jit(solution)/shard_map/ppermute | solution.py:228
  94.1 7.6 %all-to-all-done.2 = f32[16,32,256]{2,1,0:T(8,128)S(1)} async-done(((f32[16,32,256]{2,1,0:T(8,128)}), f32[16,32,256]{2,1,0:T(8,128)S(1)}, u32[]{:S(2)}, u32[]{:S(2)}) %all-to-all-start.2) | async-done | bytes 524320 | tf_op jit(solution)/shard_map/all_to_all | solution.py:274
  101.8 0.6 broadcast_multiply_fusion
  (13 shorter events, 0.2 us)
Async XLA Ops:
  3.1 8.9 %collective-permute-start = (f32[160,128]{1,0:T(8,128)}, f32[160,128]{1,0:T(8,128)S(1)}, u32[]{:S(2)}, u32[]{:S(2)}) collective-permute-start(f32[160,128]{1,0:T(8,128)} %get-tuple-element.31.after_ref), channel_id=1, source_target_pairs={{0,1},{1,0},{2,3},{3,2},{4,5},{5,4},{6,7},{7,6},{8,9},{9,8},{10,11... | collective-permute-start | bytes 245768 | tf_op jit(solution)/shard_map/ppermute | solution.py:228
  5.3 6.6 %copy-start.1 = (f32[256]{0:T(256)S(1)}, f32[256]{0:T(256)}, u32[]{:S(2)}) copy-start(f32[256]{0:T(256)} %param.6) | copy-start | bytes 3076
  5.3 6.6 %copy-start = (f32[160,128]{1,0:T(8,128)S(1)}, f32[160,128]{1,0:T(8,128)}, u32[]{:S(2)}) copy-start(f32[160,128]{1,0:T(8,128)} %get-tuple-element.32) | copy-start | bytes 245764
  5.3 39.0 %all-to-all-start = ((f32[16,264,128]{2,1,0:T(8,128)}), f32[16,264,128]{2,1,0:T(8,128)S(1)}, u32[]{:S(2)}, u32[]{:S(2)}) async-start(f32[16,264,128]{2,1,0:T(8,128)} %gate.1), calls=%async_computation | async-start | bytes 4325376 | tf_op jit(solution)/shard_map/all_to_all | solution.py:253
  12.0 9.7 %collective-permute-start.2 = (f32[1,168,256]{2,1,0:T(8,128)S(1)}, f32[1,168,256]{2,1,0:T(8,128)S(1)}, u32[]{:S(2)}, u32[]{:S(2)}) collective-permute-start(f32[1,168,256]{2,1,0:T(8,128)S(1)} %fusion.1), channel_id=1, source_target_pairs={{0,16},{16,32},{32,48},{48,64},{64,80},{80,96},{96,112},{112,0},{1... | collective-permute-start | bytes 516104 | tf_op jit(solution)/shard_map/ppermute | solution.py:238
  13.7 8.0 %collective-permute-start.3 = (f32[1,168,256]{2,1,0:T(8,128)S(1)}, f32[1,168,256]{2,1,0:T(8,128)S(1)}, u32[]{:S(2)}, u32[]{:S(2)}) collective-permute-start(f32[1,168,256]{2,1,0:T(8,128)S(1)} %fusion.1), channel_id=1, source_target_pairs={{0,112},{16,0},{32,16},{48,32},{64,48},{80,64},{96,80},{112,96},{1... | collective-permute-start | bytes 516104 | tf_op jit(solution)/shard_map/ppermute | solution.py:238
  17.8 11.7 %collective-permute-start.1 = (f32[1,168,256]{2,1,0:T(8,128)S(1)}, f32[1,168,256]{2,1,0:T(8,128)S(1)}, u32[]{:S(2)}, u32[]{:S(2)}) collective-permute-start(f32[1,168,256]{2,1,0:T(8,128)S(1)} %fusion.1), channel_id=1, source_target_pairs={{0,64},{16,80},{32,96},{48,112},{64,0},{80,16},{96,32},{112,48},{1... | collective-permute-start | bytes 516104 | tf_op jit(solution)/shard_map/ppermute | solution.py:238
  21.8 13.2 %collective-permute-start.4 = (f32[2,168,256]{2,1,0:T(8,128)S(1)}, f32[2,168,256]{2,1,0:T(8,128)S(1)}, u32[]{:S(2)}, u32[]{:S(2)}) collective-permute-start(f32[2,168,256]{2,1,0:T(8,128)S(1)} %get-tuple-element.44), channel_id=1, source_target_pairs={{0,32},{16,48},{32,64},{48,80},{64,96},{80,112},{96,0},{112,16},{1... | collective-permute-start | bytes 1032200 | tf_op jit(solution)/shard_map/ppermute | solution.py:238
  22.9 16.1 %collective-permute-start.5 = (f32[2,168,256]{2,1,0:T(8,128)S(1)}, f32[2,168,256]{2,1,0:T(8,128)S(1)}, u32[]{:S(2)}, u32[]{:S(2)}) collective-permute-start(f32[2,168,256]{2,1,0:T(8,128)S(1)} %get-tuple-element.43), channel_id=1, source_target_pairs={{0,96},{16,112},{32,0},{48,16},{64,32},{80,48},{96,64},{112,80},{1... | collective-permute-start | bytes 1032200 | tf_op jit(solution)/shard_map/ppermute | solution.py:238
  39.0 10.0 %collective-permute-start.6 = (f32[8,168,256]{2,1,0:T(8,128)S(1)}, f32[8,168,256]{2,1,0:T(8,128)}, u32[]{:S(2)}, u32[]{:S(2)}) collective-permute-start(f32[8,168,256]{2,1,0:T(8,128)S(1)} %constant_dynamic-update-slice_fusion.cols_ref), channel_id=1, source_target_pairs={{0,2},{2,0},{1,3},{3,1},{4,6},{6,4},{5,7},{7,5},{8,10},{10,8},{9,1... | collective-permute-start | bytes 4128776 | tf_op jit(solution)/shard_map/ppermute | solution.py:228
  83.4 18.3 %all-to-all-start.2 = ((f32[16,32,256]{2,1,0:T(8,128)}), f32[16,32,256]{2,1,0:T(8,128)S(1)}, u32[]{:S(2)}, u32[]{:S(2)}) async-start(f32[16,32,256]{2,1,0:T(8,128)} %get-tuple-element.41), calls=%async_computation.2 | async-start | bytes 1048576 | tf_op jit(solution)/shard_map/all_to_all | solution.py:274
  90.3 3.9 %collective-permute-start.7 = (f32[1,128]{1,0:T(1,128)S(1)}, f32[1,128]{1,0:T(1,128)S(1)}, u32[]{:S(2)}, u32[]{:S(2)}) collective-permute-start(f32[1,128]{1,0:T(1,128)S(1)} %get-tuple-element.42), channel_id=1, source_target_pairs={{0,1},{1,0},{2,3},{3,2},{4,5},{5,4},{6,7},{7,6},{8,9},{9,8},{10,11... | collective-permute-start | bytes 1544 | tf_op jit(solution)/shard_map/ppermute | solution.py:228
